TPU v7x, 32 devices: a whole 2x2x4 slice. The times are simulated.
32 devices in a mesh: row: 4 (over y, x), col: 8 (over z, core).
Axes of the slice: x: 2, y: 2, z: 4, core: 2. Of those that a mesh axis runs over, the one named last changes fastest.
Arguments:
- state: float32 [3072, 3072], P('col', 'row'), may hold values from -300 to 300
- noise: float32 [3072, 3072], P('col', 'row'), may hold values from -6 to 6
- mod_shift: float32 [3072], P('col'), may hold values from -3 to 3
- mod_scale: float32 [3072], P('col'), may hold values from -2.5 to 2.5
- mod_gate: float32 [3072], P('col'), may hold values from 0.3 to 3
- w_in: bfloat16 [3072, 12288], P('row', 'col'), may hold values from -0.109375 to 0.109375
- b_in: float32 [12288], P('col'), may hold values from -3 to 3
- w_out: bfloat16 [3072, 12288], P('col', 'row'), may hold values from -0.0546875 to 0.0546875
- b_out: float32 [3072], P('col'), may hold values from -2.5 to 2.5
Outputs:
- purified: float32 [3072, 3072], P('col', 'row')
- predicted: float32 [3072, 3072], P('col', 'row')
All inputs are finite; a program needn't handle non-finite values.
Results may differ from a plain program's by a relative error of at most 0.00049.
Values may be sent and summed in bfloat16 or wider, within the bound.
A program may use at most 128 MiB of HBM per device.

v0:
```python
import math
import jax
import jax.numpy as jnp
from jax import lax
from jax.sharding import PartitionSpec as P

D = 3072
beta_now = 2.09
step_width = 0.02
sigma_now = 0.322


def on_device(state, noise, mod_shift, mod_scale, mod_gate, w_in, b_in, w_out, b_out):
    w_in_all = lax.all_gather(w_in, "row", axis=0, tiled=True)
    w_out_all = lax.all_gather(w_out, "row", axis=1, tiled=True)
    col_sums, squares = lax.psum((jnp.sum(state, axis=0), jnp.sum(state * state, axis=0)), "col")
    center = col_sums / D
    spread = squares / D - center * center
    normed = (
        (state - center[None, :]) * lax.rsqrt(spread[None, :] + 1e-06) * (1.0 + mod_scale[:, None])
        + mod_shift[:, None]
    ).astype(jnp.bfloat16)
    normed_all = lax.all_gather(normed, "col", axis=0, tiled=True)
    pre_act = lax.dot_general(
        w_in_all, normed_all, (((0,), (0,)), ((), ())), preferred_element_type=jnp.float32
    )
    hidden = jax.nn.gelu(pre_act + b_in[:, None], approximate=True).astype(jnp.bfloat16)
    hidden_all = lax.all_gather(hidden, "col", axis=0, tiled=True)
    mixed_out = jnp.dot(w_out_all, hidden_all, preferred_element_type=jnp.float32)
    branch = mixed_out + b_out[:, None]
    predicted = state + mod_gate[:, None] * branch
    purified = (
        state * (1.0 + 0.5 * beta_now * step_width)
        - beta_now * step_width / sigma_now * predicted
        + math.sqrt(beta_now * step_width) * noise
    )
    return (purified, predicted)


def solution(mesh):
    in_specs = (
        P("col", "row"),
        P("col", "row"),
        P("col"),
        P("col"),
        P("col"),
        P("row", "col"),
        P("col"),
        P("col", "row"),
        P("col"),
    )
    out_specs = (P("col", "row"), P("col", "row"))
    return jax.shard_map(
        on_device, mesh=mesh, in_specs=in_specs, out_specs=out_specs, check_vma=False
    )
```

profile of v0, /device:TPU:0, one launch (start us, length us, event | category | flops | bytes accessed | tf_op | source)
XLA Modules:
  0.0 473.4 jit_solution(9994325539912814488)
XLA Ops:
  7.2 0.0 all-gather.5.cloned.1.call-start
  7.2 0.7 broadcast_add_fusion
  7.9 1.4 fusion.11
  9.3 18.3 %all-reduce = (f32[768]{0:T(1024)S(1)}, f32[768]{0:T(1024)S(1)}) all-reduce(f32[768]{0:T(1024)S(1)} %get-tuple-element.5, f32[768]{0:T(1024)S(1)} %get-tuple-element.4), channel_id=1, replica_groups=mesh['row'=4,'col'=8] {'col'}, use_global_device_ids=true, to_apply=%region_3.0 | all-reduce | flops 1536 | bytes 12288 | tf_op jit(solution)/shard_map/psum | solution.py:16
  27.7 2.3 add_convert_fusion
  29.9 0.0 all-gather.5.cloned.1.call-update
  30.0 0.0 copy-start.2
  30.0 0.0 all-gather.7.cloned.1.call-start
  30.0 0.7 all-gather.7.cloned.1.call-update
  30.7 0.0 all-gather.11.cloned.1.call-start
  30.8 0.7 all-gather.11.cloned.1.call-update
  31.5 0.0 all-gather.9.cloned.1.call-start
  31.5 48.5 %all-gather.5.cloned.1.call-done = bf16[3072,768]{1,0:T(8,128)(2,1)} async-done(((bf16[384,768]{1,0:T(8,128)(2,1)}), bf16[3072,768]{1,0:T(8,128)(2,1)}) %all-gather.5.cloned.1.call-update) | async-done | bytes 4718608 | tf_op jit(solution)/shard_map/all_gather | solution.py:23
  80.1 97.0 %all-gather.7.cloned.1.call-done = bf16[3072,1536]{1,0:T(8,128)(2,1)} async-done(((bf16[768,1536]{1,0:T(8,128)(2,1)}), bf16[3072,1536]{1,0:T(8,128)(2,1)}) %all-gather.7.cloned.1.call-update) | async-done | bytes 9437200 | tf_op jit(solution)/shard_map/all_gather | solution.py:14
  177.1 0.0 copy-done.2
  177.1 13.7 %fusion.7 = bf16[1536,768]{0,1:T(8,128)(2,1)} fusion(bf16[3072,768]{1,0:T(8,128)(2,1)} %all-gather.5.cloned.1.call-done, bf16[3072,1536]{1,0:T(8,128)(2,1)} %all-gather.7.cloned.1.call-done, f32[1536]{0:T(1024)S(1)} %copy-done.2), kind=kOutput, calls=%fused_computation.8 | convolution fusion | flops 7259553792 | bytes 16521216 | tf_op jit(solution)/shard_map/dot_general | solution.py:24
  190.7 0.0 copy-start
  190.7 0.0 copy-start.1
  190.7 0.0 all-gather.9.cloned.1.call-update
  190.8 1.3 copy-done
  192.1 0.0 copy-start.3
  192.1 0.0 copy-start.4
  192.1 0.4 copy.11
  192.5 0.0 copy-done.1
  192.5 0.4 copy.13
  192.9 82.4 %all-gather.11.cloned.1.call-done = bf16[384,12288]{1,0:T(8,128)(2,1)} async-done(((bf16[384,3072]{1,0:T(8,128)(2,1)}), bf16[384,12288]{1,0:T(8,128)(2,1)}) %all-gather.11.cloned.1.call-update) | async-done | bytes 9437200 | tf_op jit(solution)/shard_map/all_gather | solution.py:15
  275.3 169.8 %all-gather.9.cloned.1.call-done = bf16[12288,768]{0,1:T(8,128)(2,1)} async-done(((bf16[1536,768]{0,1:T(8,128)(2,1)}), bf16[12288,768]{0,1:T(8,128)(2,1)}) %all-gather.9.cloned.1.call-update) | async-done | bytes 18874384 | tf_op jit(solution)/shard_map/all_gather | solution.py:28
  445.1 0.0 copy-done.3
  445.1 0.0 copy-done.4
  445.1 17.8 %multiply_add_fusion = (f32[384,768]{0,1:T(8,128)}, f32[384,768]{0,1:T(8,128)S(1)}) fusion(f32[384,768]{0,1:T(8,128)S(1)} %copy.13, f32[384,768]{0,1:T(8,128)S(1)} %copy.11, f32[384]{0:T(512)S(1)} %copy-done.3, bf16[12288,768]{0,1:T(8,128)(2,1)} %all-gather.9.cloned.1.call-done, bf16[384,12288]{1,0:T(8,128)(2,1)} %all-gather.11.cloned.1.call-done, ...), kind=kOutput, calls=%fused_computation.13 | convolution fusion | flops 7250116608 | bytes 33033216 | tf_op jit(solution)/shard_map/dot_general | solution.py:29
  462.8 2.7 copy.14
  465.5 1.4 copy.15
  (1 shorter events, 0.0 us)
Async XLA Ops:
  7.2 72.9 %all-gather.5.cloned.1.call-start = ((), (), s32[]{:S(2)}) async-start(), calls=%async_computation | async-start | bytes 5308416 | tf_op jit(solution)/shard_map/all_gather | solution.py:23
  30.0 147.1 %copy-start.2 = (f32[1536]{0:T(1024)S(1)}, f32[1536]{0:T(1024)}, u32[]{:S(2)}) copy-start(f32[1536]{0:T(1024)} %param.15) | copy-start | bytes 18436
  30.0 147.1 %all-gather.7.cloned.1.call-start = ((), (), s32[]{:S(2)}) async-start(), calls=%async_computation.1 | async-start | bytes 11796480 | tf_op jit(solution)/shard_map/all_gather | solution.py:14
  30.7 244.6 %all-gather.11.cloned.1.call-start = ((), (), s32[]{:S(2)}) async-start(), calls=%async_computation.3 | async-start | bytes 11796480 | tf_op jit(solution)/shard_map/all_gather | solution.py:15
  31.5 413.6 %all-gather.9.cloned.1.call-start = ((), (), s32[]{:S(2)}) async-start(), calls=%async_computation.2 | async-start | bytes 21233664 | tf_op jit(solution)/shard_map/all_gather | solution.py:28
  190.7 1.4 copy-start
  190.7 1.8 copy-start.1
  192.1 253.0 %copy-start.3 = (f32[384]{0:T(512)S(1)}, f32[384]{0:T(512)}, u32[]{:S(2)}) copy-start(f32[384]{0:T(512)} %param.17) | copy-start | bytes 4612
  192.1 253.0 %copy-start.4 = (f32[384]{0:T(512)S(1)}, f32[384]{0:T(512)}, u32[]{:S(2)}) copy-start(f32[384]{0:T(512)} %param.13) | copy-start | bytes 4612
Sparse Core Ops, SparseCore 0:
  30.1 49.9 all-gather.4
  81.9 95.1 all-gather.6
  178.9 96.3 all-gather.10
  276.8 168.2 all-gather.8
where the time goes:
time: 474 us; the launch traced here: 473 us
  waiting for transfers between devices  399 us (84%)
  matrix products  31.4 us (7%)
  blocking collectives  18.3 us (4%)
  between operations  13.8 us (3%)
  local copies, waits for them, and re-layouts  6.13 us (1%)
    all_gather x1, waiting for transfers between devices, on_device(): hidden_all = lax.all_gather(hidden, 'col', axis=0, tiled=True)  170 us
    all_gather x1, waiting for transfers between devices, on_device(): w_in_all = lax.all_gather(w_in, 'row', axis=0, tiled=True)  97 us
    all_gather x1, waiting for transfers between devices, on_device(): w_out_all = lax.all_gather(w_out, 'row', axis=1, tiled=True)  82.4 us
    all_gather x1, waiting for transfers between devices, on_device(): normed_all = lax.all_gather(normed, 'col', axis=0, tiled=True)  48.5 us
    psum x1, blocking collectives, on_device(): lax.psum((jnp.sum(state, axis=0), jnp.sum(state * state, axis=0)), 'col')  18.3 us
    dot_general x1, matrix products, on_device(): jnp.dot(w_out_all, hidden_all, preferred_element_type=jnp.float32)  17.8 us
    dot_general x1, matrix products, on_device(): lax.dot_general(w_in_all, normed_all, (((0,), (0,)), ((), ())), preferred...  13.7 us
  transfers between devices with their start and end apart: 4, of which 4 were waited for; matrix products, arithmetic and copies ran while one was open for 3% of the time, Pallas kernels for 0%

commit v1 on v0

--- a/solution.py
+++ b/solution.py
@@ -10,6 +10,17 @@
 sigma_now = 0.322
 
 
+def turned_line(shard, axis, d):
+    size = lax.axis_size(axis)
+    route = [(i, (i + 1) % size) for i in range(size)]
+    blocks = [shard]
+    for stride in range(1, size):
+        blocks = [lax.ppermute(blocks[0], axis, route), *blocks]
+    result = jnp.concatenate(blocks, axis=d)
+    shift = (lax.axis_index(axis) + 1) * blocks[-1].shape[d]
+    return jnp.roll(result, shift, axis=d)
+
+
 def on_device(state, noise, mod_shift, mod_scale, mod_gate, w_in, b_in, w_out, b_out):
     w_in_all = lax.all_gather(w_in, "row", axis=0, tiled=True)
     w_out_all = lax.all_gather(w_out, "row", axis=1, tiled=True)
@@ -20,7 +31,7 @@
         (state - center[None, :]) * lax.rsqrt(spread[None, :] + 1e-06) * (1.0 + mod_scale[:, None])
         + mod_shift[:, None]
     ).astype(jnp.bfloat16)
-    normed_all = lax.all_gather(normed, "col", axis=0, tiled=True)
+    normed_all = turned_line(normed, "col", 0)
     pre_act = lax.dot_general(
         w_in_all, normed_all, (((0,), (0,)), ((), ())), preferred_element_type=jnp.float32
     )

time: 474 us -> 406 us (0.86)
  waiting for transfers between devices: 399 us -> 315 us
  local copies, waits for them, and re-layouts: 6.13 us -> 24.1 us
    all_gather x1, waiting for transfers between devices: 97 us -> 0.01 us  [on_device(): w_in_all = lax.all_gather(w_in, 'row', axis=0, tiled=True)]
    ppermute x0 -> x7, waiting for transfers between devices: none -> 78.1 us  [turned_line(): blocks = [lax.ppermute(blocks[0], axis, route), *blocks]]
    all_gather x1 -> x0, waiting for transfers between devices: 48.5 us -> none  [on_device(): normed_all = lax.all_gather(normed, 'col', axis=0, tiled=True)]
    unnamed x14 -> x34, local copies, waits for them, and re-layouts: 6.13 us -> 24.1 us
    all_gather x1, waiting for transfers between devices: 82.4 us -> 65.5 us  [on_device(): w_out_all = lax.all_gather(w_out, 'row', axis=1, tiled=True)]
  transfers between devices with their start and end apart: 4 -> 10, of which waited for: 4 -> 9; matrix products, arithmetic and copies ran while one was open for 3% -> 9% of each run, Pallas kernels for 0% -> 0%
where the time goes in v1:
time: 406 us; the launch traced here: 405 us
  waiting for transfers between devices  315 us (78%)
  matrix products  31.5 us (8%)
  local copies, waits for them, and re-layouts  24.1 us (6%)
  blocking collectives  18.3 us (5%)
  between operations  13.9 us (3%)
    all_gather x1, waiting for transfers between devices, on_device(): hidden_all = lax.all_gather(hidden, 'col', axis=0, tiled=True)  170 us
    ppermute x7, waiting for transfers between devices, turned_line(): blocks = [lax.ppermute(blocks[0], axis, route), *blocks]  78.1 us
    all_gather x1, waiting for transfers between devices, on_device(): w_out_all = lax.all_gather(w_out, 'row', axis=1, tiled=True)  65.5 us
    unnamed x34, local copies, waits for them, and re-layouts  24.1 us
    psum x1, blocking collectives, on_device(): lax.psum((jnp.sum(state, axis=0), jnp.sum(state * state, axis=0)), 'col')  18.3 us
    dot_general x1, matrix products, on_device(): jnp.dot(w_out_all, hidden_all, preferred_element_type=jnp.float32)  17.8 us
    dot_general x1, matrix products, on_device(): lax.dot_general(w_in_all, normed_all, (((0,), (0,)), ((), ())), preferred...  13.7 us
  transfers between devices with their start and end apart: 10, of which 9 were waited for; matrix products, arithmetic and copies ran while one was open for 9% of the time, Pallas kernels for 0%

profile of v1, /device:TPU:0, one launch (start us, length us, event | category | flops | bytes accessed | tf_op | source)
XLA Modules:
  0.0 405.5 jit_solution(13741308397192889402)
XLA Ops:
  7.2 0.0 all-gather.4.cloned.1.call-start
  7.2 0.7 all-gather.4.cloned.1.call-update
  7.9 0.0 all-gather.8.cloned.1.call-start
  8.0 0.7 all-gather.8.cloned.1.call-update
  8.7 0.0 all-gather.6.cloned.1.call-start
  8.7 0.1 fusion.16
  8.9 18.3 %all-reduce = (f32[768]{0:T(1024)S(1)}, f32[768]{0:T(1024)S(1)}) all-reduce(f32[768]{0:T(1024)S(1)} %get-tuple-element.5, f32[768]{0:T(1024)S(1)} %get-tuple-element.4), channel_id=1, replica_groups=mesh['row'=4,'col'=8] {'col'}, use_global_device_ids=true, to_apply=%region_3.0 | all-reduce | flops 1536 | bytes 12288 | tf_op jit(solution)/shard_map/psum | solution.py:27
  27.3 0.2 add_convert_fusion
  27.5 0.1 collective-permute-start
  27.5 11.1 %collective-permute-done = bf16[384,768]{1,0:T(8,128)(2,1)S(1)} collective-permute-done((bf16[384,768]{1,0:T(8,128)(2,1)S(1)}, bf16[384,768]{1,0:T(8,128)(2,1)S(1)}, u32[]{:S(2)}, u32[]{:S(2)}) %collective-permute-start) | collective-permute-done | bytes 589856 | tf_op jit(solution)/shard_map/ppermute | solution.py:18
  38.6 0.0 collective-permute-start.1
  38.6 11.1 %collective-permute-done.1 = bf16[384,768]{1,0:T(8,128)(2,1)S(1)} collective-permute-done((bf16[384,768]{1,0:T(8,128)(2,1)S(1)}, bf16[384,768]{1,0:T(8,128)(2,1)S(1)}, u32[]{:S(2)}, u32[]{:S(2)}) %collective-permute-start.1) | collective-permute-done | bytes 589856 | tf_op jit(solution)/shard_map/ppermute | solution.py:18
  49.7 0.0 collective-permute-start.2
  49.7 11.1 %collective-permute-done.2 = bf16[384,768]{1,0:T(8,128)(2,1)S(1)} collective-permute-done((bf16[384,768]{1,0:T(8,128)(2,1)S(1)}, bf16[384,768]{1,0:T(8,128)(2,1)S(1)}, u32[]{:S(2)}, u32[]{:S(2)}) %collective-permute-start.2) | collective-permute-done | bytes 589856 | tf_op jit(solution)/shard_map/ppermute | solution.py:18
  60.8 0.0 collective-permute-start.3
  60.9 11.1 %collective-permute-done.3 = bf16[384,768]{1,0:T(8,128)(2,1)S(1)} collective-permute-done((bf16[384,768]{1,0:T(8,128)(2,1)S(1)}, bf16[384,768]{1,0:T(8,128)(2,1)S(1)}, u32[]{:S(2)}, u32[]{:S(2)}) %collective-permute-start.3) | collective-permute-done | bytes 589856 | tf_op jit(solution)/shard_map/ppermute | solution.py:18
  72.0 0.0 collective-permute-start.4
  72.0 11.1 %collective-permute-done.4 = bf16[384,768]{1,0:T(8,128)(2,1)S(1)} collective-permute-done((bf16[384,768]{1,0:T(8,128)(2,1)S(1)}, bf16[384,768]{1,0:T(8,128)(2,1)S(1)}, u32[]{:S(2)}, u32[]{:S(2)}) %collective-permute-start.4) | collective-permute-done | bytes 589856 | tf_op jit(solution)/shard_map/ppermute | solution.py:18
  83.1 0.8 copy-done.1
  83.9 11.2 %collective-permute-done.5 = bf16[384,768]{1,0:T(8,128)(2,1)} collective-permute-done((bf16[384,768]{1,0:T(8,128)(2,1)S(1)}, bf16[384,768]{1,0:T(8,128)(2,1)}, u32[]{:S(2)}, u32[]{:S(2)}) %collective-permute-start.5) | collective-permute-done | bytes 589856 | tf_op jit(solution)/shard_map/ppermute | solution.py:18
  95.1 0.0 collective-permute-start.6
  95.1 11.4 %collective-permute-done.6 = bf16[384,768]{1,0:T(8,128)(2,1)} collective-permute-done((bf16[384,768]{1,0:T(8,128)(2,1)}, bf16[384,768]{1,0:T(8,128)(2,1)}, u32[]{:S(2)}, u32[]{:S(2)}) %collective-permute-start.6) | collective-permute-done | bytes 589856 | tf_op jit(solution)/shard_map/ppermute | solution.py:18
  106.5 1.9 constant_dynamic-update-slice_fusion.15
  108.4 1.9 constant_dynamic-update-slice_fusion.14
  110.4 1.9 constant_dynamic-update-slice_fusion.13
  112.3 0.8 constant_dynamic-update-slice_fusion.12
  113.2 0.9 constant_dynamic-update-slice_fusion.11
  114.0 0.9 constant_dynamic-update-slice_fusion.10
  114.9 0.9 constant_dynamic-update-slice_fusion.9
  115.8 1.1 constant_dynamic-update-slice_fusion.8
  116.8 2.0 constant_dynamic-update-slice_fusion.7
  118.9 2.0 constant_dynamic-update-slice_fusion.6
  120.9 0.9 constant_dynamic-update-slice_fusion.5
  121.7 0.9 constant_dynamic-update-slice_fusion.4
  122.6 0.9 constant_dynamic-update-slice_fusion.3
  123.5 0.9 constant_dynamic-update-slice_fusion.2
  124.3 0.9 constant_dynamic-update-slice_fusion.1
  125.2 1.0 constant_dynamic-update-slice_fusion
  126.3 13.7 %fusion.7 = bf16[1536,768]{0,1:T(8,128)(2,1)} fusion(bf16[3072,1536]{1,0:T(8,128)(2,1)} %all-gather.4.cloned.1.call-done, bf16[6144,768]{1,0:T(8,128)(2,1)} %constant_dynamic-update-slice_fusion, s32[]{:T(128)S(6)} %select_n.14, f32[1536]{0:T(1024)} %param.15), kind=kOutput, calls=%fused_computation.8 | convolution fusion | flops 7259553792 | bytes 16523268 | tf_op jit(solution)/shard_map/dot_general | solution.py:35
  140.0 0.0 all-gather.6.cloned.1.call-update
  140.0 0.4 copy.11
  140.4 0.9 copy-done.3
  141.2 0.4 copy.13
  141.6 65.5 %all-gather.8.cloned.1.call-done = bf16[384,12288]{1,0:T(8,128)(2,1)} async-done(((bf16[384,3072]{1,0:T(8,128)(2,1)}), bf16[384,12288]{1,0:T(8,128)(2,1)}) %all-gather.8.cloned.1.call-update) | async-done | bytes 9437200 | tf_op jit(solution)/shard_map/all_gather | solution.py:26
  207.2 169.9 %all-gather.6.cloned.1.call-done = bf16[12288,768]{0,1:T(8,128)(2,1)} async-done(((bf16[1536,768]{0,1:T(8,128)(2,1)}), bf16[12288,768]{0,1:T(8,128)(2,1)}) %all-gather.6.cloned.1.call-update) | async-done | bytes 18874384 | tf_op jit(solution)/shard_map/all_gather | solution.py:39
  377.1 17.8 %multiply_add_fusion = (f32[384,768]{0,1:T(8,128)}, f32[384,768]{0,1:T(8,128)S(1)}) fusion(f32[384,768]{0,1:T(8,128)S(1)} %copy.13, f32[384,768]{0,1:T(8,128)S(1)} %copy.11, f32[384]{0:T(512)S(1)} %copy-done.6, bf16[12288,768]{0,1:T(8,128)(2,1)} %all-gather.6.cloned.1.call-done, bf16[384,12288]{1,0:T(8,128)(2,1)} %all-gather.8.cloned.1.call-done, ...), kind=kOutput, calls=%fused_computation.15 | convolution fusion | flops 7250116608 | bytes 33033216 | tf_op jit(solution)/shard_map/dot_general | solution.py:40
  394.9 2.7 copy.14
  397.6 1.4 copy.15
  (18 shorter events, 0.0 us)
Async XLA Ops:
  7.2 1.6 copy-start
  7.2 20.1 %copy-start.5 = (f32[384]{0:T(512)S(1)}, f32[384]{0:T(512)}, u32[]{:S(2)}) copy-start(f32[384]{0:T(512)} %param.12) | copy-start | bytes 4612
  7.2 20.1 %copy-start.4 = (f32[384]{0:T(512)S(1)}, f32[384]{0:T(512)}, u32[]{:S(2)}) copy-start(f32[384]{0:T(512)} %param.11) | copy-start | bytes 4612
  7.2 119.1 %all-gather.4.cloned.1.call-start = ((), (), s32[]{:S(2)}) async-start(), calls=%async_computation | async-start | bytes 11796480 | tf_op jit(solution)/shard_map/all_gather | solution.py:25
  7.9 199.2 %all-gather.8.cloned.1.call-start = ((), (), s32[]{:S(2)}) async-start(), calls=%async_computation.2 | async-start | bytes 11796480 | tf_op jit(solution)/shard_map/all_gather | solution.py:26
  8.7 368.4 %all-gather.6.cloned.1.call-start = ((), (), s32[]{:S(2)}) async-start(), calls=%async_computation.1 | async-start | bytes 21233664 | tf_op jit(solution)/shard_map/all_gather | solution.py:39
  27.5 11.2 %collective-permute-start = (bf16[384,768]{1,0:T(8,128)(2,1)S(1)}, bf16[384,768]{1,0:T(8,128)(2,1)S(1)}, u32[]{:S(2)}, u32[]{:S(2)}) collective-permute-start(bf16[384,768]{1,0:T(8,128)(2,1)S(1)} %add_convert_fusion), channel_id=1, source_target_pairs={{0,1},{1,2},{2,3},{3,4},{4,5},{5,6},{6,7},{7,0},{8,9},{9,10},{10,1... | collective-permute-start | bytes 1769480 | tf_op jit(solution)/shard_map/ppermute | solution.py:18
  38.6 11.1 %collective-permute-start.1 = (bf16[384,768]{1,0:T(8,128)(2,1)S(1)}, bf16[384,768]{1,0:T(8,128)(2,1)S(1)}, u32[]{:S(2)}, u32[]{:S(2)}) collective-permute-start(bf16[384,768]{1,0:T(8,128)(2,1)S(1)} %collective-permute-done), channel_id=1, source_target_pairs={{0,1},{1,2},{2,3},{3,4},{4,5},{5,6},{6,7},{7,0},{8,9},{9,10},{10,1... | collective-permute-start | bytes 1769480 | tf_op jit(solution)/shard_map/ppermute | solution.py:18
  49.7 11.1 %collective-permute-start.2 = (bf16[384,768]{1,0:T(8,128)(2,1)S(1)}, bf16[384,768]{1,0:T(8,128)(2,1)S(1)}, u32[]{:S(2)}, u32[]{:S(2)}) collective-permute-start(bf16[384,768]{1,0:T(8,128)(2,1)S(1)} %collective-permute-done.1), channel_id=1, source_target_pairs={{0,1},{1,2},{2,3},{3,4},{4,5},{5,6},{6,7},{7,0},{8,9},{9,10},{10,1... | collective-permute-start | bytes 1769480 | tf_op jit(solution)/shard_map/ppermute | solution.py:18
  60.8 11.1 %collective-permute-start.3 = (bf16[384,768]{1,0:T(8,128)(2,1)S(1)}, bf16[384,768]{1,0:T(8,128)(2,1)S(1)}, u32[]{:S(2)}, u32[]{:S(2)}) collective-permute-start(bf16[384,768]{1,0:T(8,128)(2,1)S(1)} %collective-permute-done.2), channel_id=1, source_target_pairs={{0,1},{1,2},{2,3},{3,4},{4,5},{5,6},{6,7},{7,0},{8,9},{9,10},{10,1... | collective-permute-start | bytes 1769480 | tf_op jit(solution)/shard_map/ppermute | solution.py:18
  72.0 11.1 %collective-permute-start.4 = (bf16[384,768]{1,0:T(8,128)(2,1)S(1)}, bf16[384,768]{1,0:T(8,128)(2,1)S(1)}, u32[]{:S(2)}, u32[]{:S(2)}) collective-permute-start(bf16[384,768]{1,0:T(8,128)(2,1)S(1)} %collective-permute-done.3), channel_id=1, source_target_pairs={{0,1},{1,2},{2,3},{3,4},{4,5},{5,6},{6,7},{7,0},{8,9},{9,10},{10,1... | collective-permute-start | bytes 1769480 | tf_op jit(solution)/shard_map/ppermute | solution.py:18
  83.1 0.8 copy-start.1
  83.9 11.2 %collective-permute-start.5 = (bf16[384,768]{1,0:T(8,128)(2,1)S(1)}, bf16[384,768]{1,0:T(8,128)(2,1)}, u32[]{:S(2)}, u32[]{:S(2)}) collective-permute-start(bf16[384,768]{1,0:T(8,128)(2,1)S(1)} %collective-permute-done.4), channel_id=1, source_target_pairs={{0,1},{1,2},{2,3},{3,4},{4,5},{5,6},{6,7},{7,0},{8,9},{9,10},{10,1... | collective-permute-start | bytes 1769480 | tf_op jit(solution)/shard_map/ppermute | solution.py:18
  95.1 11.4 %collective-permute-start.6 = (bf16[384,768]{1,0:T(8,128)(2,1)}, bf16[384,768]{1,0:T(8,128)(2,1)}, u32[]{:S(2)}, u32[]{:S(2)}) collective-permute-start(bf16[384,768]{1,0:T(8,128)(2,1)} %collective-permute-done.5), channel_id=1, source_target_pairs={{0,1},{1,2},{2,3},{3,4},{4,5},{5,6},{6,7},{7,0},{8,9},{9,10},{10,1... | collective-permute-start | bytes 1769480 | tf_op jit(solution)/shard_map/ppermute | solution.py:18
  112.3 8.6 %copy-start.2 = (bf16[384,768]{1,0:T(8,128)(2,1)S(1)}, bf16[384,768]{1,0:T(8,128)(2,1)}, u32[]{:S(2)}) copy-start(bf16[384,768]{1,0:T(8,128)(2,1)} %copy-done.1) | copy-start | bytes 1769476
  140.0 1.3 copy-start.3
  140.0 237.1 %copy-start.6 = (f32[384]{0:T(512)S(1)}, f32[384]{0:T(512)}, u32[]{:S(2)}) copy-start(f32[384]{0:T(512)} %param.17) | copy-start | bytes 4612
  140.0 237.1 %copy-start.7 = (f32[384]{0:T(512)S(1)}, f32[384]{0:T(512)}, u32[]{:S(2)}) copy-start(f32[384]{0:T(512)} %param.13) | copy-start | bytes 4612
Sparse Core Ops, SparseCore 0:
  9.9 99.0 all-gather.3
  110.8 96.3 all-gather.7
  208.8 168.2 all-gather.5
